TPU v7x, 32 devices: a whole 2x2x4 slice. The times are simulated.
32 devices in a mesh: gx: 8 (over y, x, core), gy: 4 (over z).
Axes of the slice: x: 2, y: 2, z: 4, core: 2. Of those that a mesh axis runs over, the one named last changes fastest.
Arguments:
- populations: float32 [19, 8, 256, 512], P(None, None, 'gx', 'gy'), may hold values from 0.6 to 1.4
- concentrations: float32 [2, 8, 256, 512], P(None, None, 'gx', 'gy'), may hold values from 0.3 to 3
- potential: float32 [8, 256, 512], P(None, 'gx', 'gy'), may hold values from -4 to 4
- permittivity: float32 [8, 256, 512], P(None, 'gx', 'gy'), may hold values from 0.3 to 3
- solid: int32 [8, 256, 512], P(None, 'gx', 'gy'), may hold values 0 or 1
- bead_label: int32 [8, 256, 512], P(None, 'gx', 'gy'), may hold values from 0 to 4, as said below
- bead_charge: float32 [4], replicated, may hold values from -2 to 1
- rates: float32 [5], replicated, may hold values from 0.7 to 1.9
- diffusivity: float32 [2], replicated, may hold values from 0.03 to 0.12
Outputs:
- populations_out: float32 [19, 8, 256, 512], P(None, None, 'gx', 'gy')
- concentrations_out: float32 [2, 8, 256, 512], P(None, None, 'gx', 'gy')
- potential_out: float32 [8, 256, 512], P(None, 'gx', 'gy')
Inputs may be any that keep to these rules, and one draw needn't show every extreme that they name: `solid`: 1 marks a pore-wall cell. `bead_label`: 0 marks a cell without a bead; 1 to 4 select an entry of bead_charge.
All inputs are finite; a program needn't handle non-finite values. No bound on the sum of `solid` on one device may be relied on, other than what follows from the above.
Results may differ from a plain program's by a relative error of at most 0.0001.
Values sent between devices are 32-bit elements; how exact they have to be, the bound alone decides.
A program may use at most 64 MiB of HBM per device.

v0:
```python
import jax
import jax.numpy as jnp
import numpy as np
from jax import lax
from jax.sharding import PartitionSpec as P

STEPS = 8
SWEEPS = 3


VELOCITIES = np.array(
    [
        [0, 0, 0],
        [1, 0, 0],
        [-1, 0, 0],
        [0, 1, 0],
        [0, -1, 0],
        [0, 0, 1],
        [0, 0, -1],
        [1, 1, 0],
        [-1, -1, 0],
        [1, -1, 0],
        [-1, 1, 0],
        [1, 0, 1],
        [-1, 0, -1],
        [1, 0, -1],
        [-1, 0, 1],
        [0, 1, 1],
        [0, -1, -1],
        [0, 1, -1],
        [0, -1, 1],
    ]
)
RATE_SLOTS = np.array([5, 0, 1, 5, 2, 5, 2, 5, 2, 3, 1, 3, 1, 3, 3, 3, 4, 4, 4])
FORCE_SCALE = 0.02
EXT_FIELD = 0.05
HIGHEST = lax.Precision.HIGHEST


def with_halo(block, sides, width):
    for axis, dim in sides:
        count = lax.axis_size(axis)
        forward = [(i, i + 1) for i in range(count - 1)]
        forward.append((count - 1, 0))
        backward = [(target, source) for source, target in forward]
        low = lax.ppermute(
            lax.slice_in_dim(block, block.shape[dim] - width, None, axis=dim), axis, forward
        )
        high = lax.ppermute(lax.slice_in_dim(block, 0, width, axis=dim), axis, backward)
        block = jnp.concatenate([low, block, high], axis=dim)
    return block


def lattice_weights():
    square = np.sum(VELOCITIES * VELOCITIES, axis=1)
    return np.where(square == 0, 1.0 / 3.0, np.where(square == 1, 1.0 / 18.0, 1.0 / 36.0))


def opposites():
    return [
        int(np.argmax(np.all(VELOCITIES == -VELOCITIES[member], axis=1))) for member in range(19)
    ]


def moment_matrix():
    veloc = VELOCITIES * 1.0
    along_x, along_y, along_z = (veloc[:, 0], veloc[:, 1], veloc[:, 2])
    square = along_x * along_x + along_y * along_y + along_z * along_z
    heat = 5.0 * square - 9.0
    ghost = 3.0 * square - 5.0
    normal_xx = 3.0 * along_x * along_x - square
    normal_ww = along_y * along_y - along_z * along_z
    rows = [
        np.ones(19),
        19.0 * square - 30.0,
        (21.0 * square * square - 53.0 * square + 24.0) / 2.0,
        along_x,
        heat * along_x,
        along_y,
        heat * along_y,
        along_z,
        heat * along_z,
        normal_xx,
        ghost * normal_xx,
        normal_ww,
        ghost * normal_ww,
        along_x * along_y,
        along_y * along_z,
        along_x * along_z,
        (along_y * along_y - along_z * along_z) * along_x,
        (along_z * along_z - along_x * along_x) * along_y,
        (along_x * along_x - along_y * along_y) * along_z,
    ]
    return np.stack(rows)


def relaxation(rates):
    weights = lattice_weights()
    matrix = moment_matrix()
    norms = np.sum(matrix * matrix, axis=1)
    left_side = matrix.T / norms[None, :] / weights[:, None]
    right_side = matrix * weights[None, :]
    full = jnp.concatenate([rates, jnp.ones((1,), jnp.float32)])
    strength = full[jnp.asarray(RATE_SLOTS)]
    return jnp.dot(
        jnp.asarray(left_side, jnp.float32) * strength[None, :],
        jnp.asarray(right_side, jnp.float32),
        precision=HIGHEST,
    )


def bead_density(bead_label, bead_charge):
    levels = jnp.arange(1, 5, dtype=jnp.int32)
    chosen = (bead_label[None] == levels[:, None, None, None]).astype(jnp.float32)
    return jnp.sum(chosen * bead_charge[:, None, None, None], axis=0)


def macroscopic(populations, forcing):
    weights = jnp.asarray(lattice_weights(), jnp.float32)
    carried = jnp.asarray((VELOCITIES * lattice_weights()[:, None]).T, jnp.float32)
    density = jnp.einsum("q,q...->...", weights, populations, precision=HIGHEST)
    momentum = jnp.einsum("aq,q...->a...", carried, populations, precision=HIGHEST)
    velocity = (momentum + 0.5 * forcing) / density[None]
    return (density, velocity)


def collide_cells(populations, density, velocity, forcing, relax):
    lattice = jnp.asarray(VELOCITIES, jnp.float32)
    along_u = jnp.einsum("qa,a...->q...", lattice, velocity, precision=HIGHEST)
    along_f = jnp.einsum("qa,a...->q...", lattice, forcing, precision=HIGHEST)
    speed_sq = jnp.sum(velocity * velocity, axis=0)
    work_done = jnp.sum(velocity * forcing, axis=0)
    balance = density[None] * (1.0 + 3.0 * along_u + 4.5 * along_u * along_u - 1.5 * speed_sq[None])
    source = 3.0 * (along_f - work_done[None]) + 9.0 * along_u * along_f
    shifted = populations - balance + 0.5 * source
    return populations + source - jnp.einsum("qp,p...->q...", relax, shifted, precision=HIGHEST)


def face_flux(
    here_conc,
    next_conc,
    here_pot,
    next_pot,
    here_vel,
    next_vel,
    here_open,
    next_open,
    diffusivity,
    bias,
):
    valence = jnp.asarray([1.0, -1.0], jnp.float32)[:, None, None, None]
    spread = diffusivity[:, None, None, None]
    middle = 0.5 * (here_conc + next_conc)
    drift = (next_pot - here_pot - bias)[None]
    flux = (
        -spread * (next_conc - here_conc + valence * middle * drift)
        + 0.5 * (here_vel + next_vel)[None] * middle
    )
    return flux * (here_open * next_open)[None]


def jacobi_local(pot_pad, eps_pad, source):
    centre_eps = eps_pad[:, 1:-1, 1:-1]
    centre_pot = pot_pad[:, 1:-1, 1:-1]
    neighbours = [
        (pot_pad[:, 2:, 1:-1], eps_pad[:, 2:, 1:-1]),
        (pot_pad[:, :-2, 1:-1], eps_pad[:, :-2, 1:-1]),
        (pot_pad[:, 1:-1, 2:], eps_pad[:, 1:-1, 2:]),
        (pot_pad[:, 1:-1, :-2], eps_pad[:, 1:-1, :-2]),
        (jnp.roll(centre_pot, -1, 0), jnp.roll(centre_eps, -1, 0)),
        (jnp.roll(centre_pot, 1, 0), jnp.roll(centre_eps, 1, 0)),
    ]
    numerator = source
    denominator = jnp.zeros_like(source)
    for near_pot, near_eps in neighbours:
        weight = 0.5 * (centre_eps + near_eps)
        numerator = numerator + weight * near_pot
        denominator = denominator + weight
    return numerator / denominator


def transport_local(concentrations, padded_ions, pot_pad, open_pad, diffusivity):
    conc_pad = padded_ions[:2]
    vel_pad = padded_ions[2:]
    flux = face_flux(
        conc_pad[:, :, :-1, 1:-1],
        conc_pad[:, :, 1:, 1:-1],
        pot_pad[:, :-1, 1:-1],
        pot_pad[:, 1:, 1:-1],
        vel_pad[0][:, :-1, 1:-1],
        vel_pad[0][:, 1:, 1:-1],
        open_pad[:, :-1, 1:-1],
        open_pad[:, 1:, 1:-1],
        diffusivity,
        0.0,
    )
    change = flux[:, :, 1:, :] - flux[:, :, :-1, :]
    flux = face_flux(
        conc_pad[:, :, 1:-1, :-1],
        conc_pad[:, :, 1:-1, 1:],
        pot_pad[:, 1:-1, :-1],
        pot_pad[:, 1:-1, 1:],
        vel_pad[1][:, 1:-1, :-1],
        vel_pad[1][:, 1:-1, 1:],
        open_pad[:, 1:-1, :-1],
        open_pad[:, 1:-1, 1:],
        diffusivity,
        0.0,
    )
    change = change + (flux[..., 1:] - flux[..., :-1])
    centre_pot = pot_pad[:, 1:-1, 1:-1]
    centre_vel = vel_pad[2][:, 1:-1, 1:-1]
    centre_open = open_pad[:, 1:-1, 1:-1]
    flux = face_flux(
        concentrations,
        jnp.roll(concentrations, -1, 1),
        centre_pot,
        jnp.roll(centre_pot, -1, 0),
        centre_vel,
        jnp.roll(centre_vel, -1, 0),
        centre_open,
        jnp.roll(centre_open, -1, 0),
        diffusivity,
        EXT_FIELD,
    )
    change = change + (flux - jnp.roll(flux, 1, 1))
    return concentrations - change


def stream_whole(post):
    padded = with_halo(post, (("gx", 2), ("gy", 3)), 1)
    tile_x = post.shape[2]
    tile_y = post.shape[3]
    rows = []
    for member in range(19):
        step_x = int(VELOCITIES[member][0])
        step_y = int(VELOCITIES[member][1])
        step_z = int(VELOCITIES[member][2])
        piece = padded[member][
            :, 1 - step_x : 1 - step_x + tile_x, 1 - step_y : 1 - step_y + tile_y
        ]
        rows.append(jnp.roll(piece, step_z, 0))
    return rows


def local(
    populations,
    concentrations,
    potential,
    permittivity,
    solid,
    bead_label,
    bead_charge,
    rates,
    diffusivity,
):
    depth = 1
    relax = relaxation(rates)
    open_cells = (1 - solid).astype(jnp.float32)
    bead_field = bead_density(bead_label, bead_charge)
    medium = with_halo(jnp.stack([permittivity, open_cells]), (("gx", 2), ("gy", 3)), depth)
    eps_wide = medium[0]
    open_pad = medium[1]
    opposite = opposites()
    tile_x = populations.shape[2]
    tile_y = populations.shape[3]

    def advance(repeat, state):
        populations, concentrations, potential = state
        charge_field = open_cells * (concentrations[0] - concentrations[1]) + bead_field
        for sweep_count in range(SWEEPS + 1):
            pot_pad = with_halo(potential, (("gx", 1), ("gy", 2)), 1)
            if sweep_count < SWEEPS:
                potential = jacobi_local(pot_pad, eps_wide, charge_field)
        electric = jnp.stack(
            [
                -0.5 * (pot_pad[:, 2:, 1:-1] - pot_pad[:, :-2, 1:-1]),
                -0.5 * (pot_pad[:, 1:-1, 2:] - pot_pad[:, 1:-1, :-2]),
                -0.5 * (jnp.roll(potential, -1, 0) - jnp.roll(potential, 1, 0)) + EXT_FIELD,
            ]
        )
        forcing = FORCE_SCALE * (charge_field * open_cells)[None] * electric
        density, velocity = macroscopic(populations, forcing)
        padded_ions = with_halo(
            jnp.concatenate([concentrations, velocity]), (("gx", 2), ("gy", 3)), 1
        )
        new_conc = transport_local(concentrations, padded_ions, pot_pad, open_pad, diffusivity)
        post = collide_cells(populations, density, velocity, forcing, relax)
        moved_all = stream_whole(post)
        rows = []
        for member in range(19):
            step_x = int(VELOCITIES[member][0])
            step_y = int(VELOCITIES[member][1])
            step_z = int(VELOCITIES[member][2])
            source_open = jnp.roll(
                open_pad[:, 1 - step_x : 1 - step_x + tile_x, 1 - step_y : 1 - step_y + tile_y],
                step_z,
                0,
            )
            rows.append(jnp.where(source_open > 0.5, moved_all[member], post[opposite[member]]))
        populations = jnp.where(open_cells[None] > 0.5, jnp.stack(rows), populations)
        return (populations, new_conc, potential)

    return lax.fori_loop(0, STEPS, advance, (populations, concentrations, potential))


def solution(mesh):
    in_specs = (
        P(None, None, "gx", "gy"),
        P(None, None, "gx", "gy"),
        P(None, "gx", "gy"),
        P(None, "gx", "gy"),
        P(None, "gx", "gy"),
        P(None, "gx", "gy"),
        P(),
        P(),
        P(),
    )
    out_specs = (P(None, None, "gx", "gy"), P(None, None, "gx", "gy"), P(None, "gx", "gy"))
    return jax.shard_map(local, mesh=mesh, in_specs=in_specs, out_specs=out_specs, check_vma=False)
```

profile of v0, /device:TPU:0, one launch (start us, length us, event | category | flops | bytes accessed | tf_op | source)
XLA Modules:
  0.0 1196.6 jit_solution(4489901311977884107)
XLA Ops:
  12.1 7.8 collective-permute-done.26
  19.8 6.2 collective-permute-done.27
  33.6 1161.1 %while.19 = (s32[]{:T(128)}, f32[19,8,32,128]{3,2,1,0:T(8,128)S(1)}, f32[2,8,32,128]{3,2,1,0:T(8,128)S(1)}, f32[8,32,128]{2,1,0:T(8,128)S(1)}, f32[8,32,128]{2,1...) while((s32[]{:T(128)}, ...), condition=%wide.region_4.5_spmd.clone.clone, body=%wide.region_1.4_spmd.sunk.clone.clone.sunk | while | flops 246829152 | bytes 153202576 | solution.py:304
  59.8 4.3 fusion.222
  121.1 4.5 collective-permute-done.14
  137.8 4.2 fusion.249
  188.5 6.6 pad_maximum_fusion.87
  201.8 4.3 fusion.222
  279.1 4.2 fusion.249
  330.4 6.6 pad_maximum_fusion.87
  343.8 4.3 fusion.222
  472.5 6.6 pad_maximum_fusion.87
  485.9 4.3 fusion.222
  614.5 6.6 pad_maximum_fusion.87
  627.9 4.3 fusion.222
  756.6 6.6 pad_maximum_fusion.87
  770.0 4.3 fusion.222
  898.6 6.6 pad_maximum_fusion.87
  912.0 4.3 fusion.222
  989.3 4.2 fusion.249
  1040.7 6.6 pad_maximum_fusion.87
  1054.1 4.3 fusion.222
  1131.4 4.2 fusion.249
  1182.7 6.6 pad_maximum_fusion.87
  (2088 shorter events, 1041.5 us)
Async XLA Ops:
  129.1 17.9 %collective-permute-start.20 = (f32[5,8,1,128]{3,2,1,0:T(1,128)S(1)}, f32[5,8,1,128]{3,2,1,0:T(1,128)S(1)}, u32[]{:S(2)}, u32[]{:S(2)}) collective-permute-start(f32[5,8,1,128]{3,2,1,0:T(1,128)S(1)} %get-tuple-element.1226), channel_id=1, source_target_pairs={{4,0},{8,4},{12,8},{16,12},{20,16},{24,20},{28,24},{0,28},{5,1},{9... | collective-permute-start | bytes 61448 | tf_op jit(solution)/shard_map/while/body/eval_jaxpr/ppermute | solution.py:49
  144.4 21.6 %collective-permute-start.16 = (f32[19,8,1,128]{3,2,1,0:T(1,128)}, f32[19,8,1,128]{3,2,1,0:T(1,128)}, u32[]{:S(2)}, u32[]{:S(2)}) collective-permute-start(f32[19,8,1,128]{3,2,1,0:T(1,128)} %get-tuple-element.1183), channel_id=1, source_target_pairs={{4,0},{8,4},{12,8},{16,12},{20,16},{24,20},{28,24},{0,28},{5,1},{9... | collective-permute-start | bytes 233480 | tf_op jit(solution)/shard_map/while/body/eval_jaxpr/ppermute | solution.py:49
  147.1 19.0 %collective-permute-start.17 = (f32[19,8,1,128]{3,2,1,0:T(1,128)}, f32[19,8,1,128]{3,2,1,0:T(1,128)}, u32[]{:S(2)}, u32[]{:S(2)}) collective-permute-start(f32[19,8,1,128]{3,2,1,0:T(1,128)} %get-tuple-element.1184), channel_id=1, source_target_pairs={{0,4},{4,8},{8,12},{12,16},{16,20},{20,24},{24,28},{28,0},{1,5},{5... | collective-permute-start | bytes 233480 | tf_op jit(solution)/shard_map/while/body/eval_jaxpr/ppermute | solution.py:46
  270.5 17.9 %collective-permute-start.20 = (f32[5,8,1,128]{3,2,1,0:T(1,128)S(1)}, f32[5,8,1,128]{3,2,1,0:T(1,128)S(1)}, u32[]{:S(2)}, u32[]{:S(2)}) collective-permute-start(f32[5,8,1,128]{3,2,1,0:T(1,128)S(1)} %get-tuple-element.1226), channel_id=1, source_target_pairs={{4,0},{8,4},{12,8},{16,12},{20,16},{24,20},{28,24},{0,28},{5,1},{9... | collective-permute-start | bytes 61448 | tf_op jit(solution)/shard_map/while/body/eval_jaxpr/ppermute | solution.py:49
  285.7 22.3 %collective-permute-start.16 = (f32[19,8,1,128]{3,2,1,0:T(1,128)}, f32[19,8,1,128]{3,2,1,0:T(1,128)}, u32[]{:S(2)}, u32[]{:S(2)}) collective-permute-start(f32[19,8,1,128]{3,2,1,0:T(1,128)} %get-tuple-element.1183), channel_id=1, source_target_pairs={{4,0},{8,4},{12,8},{16,12},{20,16},{24,20},{28,24},{0,28},{5,1},{9... | collective-permute-start | bytes 233480 | tf_op jit(solution)/shard_map/while/body/eval_jaxpr/ppermute | solution.py:49
  288.4 19.6 %collective-permute-start.17 = (f32[19,8,1,128]{3,2,1,0:T(1,128)}, f32[19,8,1,128]{3,2,1,0:T(1,128)}, u32[]{:S(2)}, u32[]{:S(2)}) collective-permute-start(f32[19,8,1,128]{3,2,1,0:T(1,128)} %get-tuple-element.1184), channel_id=1, source_target_pairs={{0,4},{4,8},{8,12},{12,16},{16,20},{20,24},{24,28},{28,0},{1,5},{5... | collective-permute-start | bytes 233480 | tf_op jit(solution)/shard_map/while/body/eval_jaxpr/ppermute | solution.py:46
  412.5 17.9 %collective-permute-start.20 = (f32[5,8,1,128]{3,2,1,0:T(1,128)S(1)}, f32[5,8,1,128]{3,2,1,0:T(1,128)S(1)}, u32[]{:S(2)}, u32[]{:S(2)}) collective-permute-start(f32[5,8,1,128]{3,2,1,0:T(1,128)S(1)} %get-tuple-element.1226), channel_id=1, source_target_pairs={{4,0},{8,4},{12,8},{16,12},{20,16},{24,20},{28,24},{0,28},{5,1},{9... | collective-permute-start | bytes 61448 | tf_op jit(solution)/shard_map/while/body/eval_jaxpr/ppermute | solution.py:49
  427.7 22.3 %collective-permute-start.16 = (f32[19,8,1,128]{3,2,1,0:T(1,128)}, f32[19,8,1,128]{3,2,1,0:T(1,128)}, u32[]{:S(2)}, u32[]{:S(2)}) collective-permute-start(f32[19,8,1,128]{3,2,1,0:T(1,128)} %get-tuple-element.1183), channel_id=1, source_target_pairs={{4,0},{8,4},{12,8},{16,12},{20,16},{24,20},{28,24},{0,28},{5,1},{9... | collective-permute-start | bytes 233480 | tf_op jit(solution)/shard_map/while/body/eval_jaxpr/ppermute | solution.py:49
  430.4 19.7 %collective-permute-start.17 = (f32[19,8,1,128]{3,2,1,0:T(1,128)}, f32[19,8,1,128]{3,2,1,0:T(1,128)}, u32[]{:S(2)}, u32[]{:S(2)}) collective-permute-start(f32[19,8,1,128]{3,2,1,0:T(1,128)} %get-tuple-element.1184), channel_id=1, source_target_pairs={{0,4},{4,8},{8,12},{12,16},{16,20},{20,24},{24,28},{28,0},{1,5},{5... | collective-permute-start | bytes 233480 | tf_op jit(solution)/shard_map/while/body/eval_jaxpr/ppermute | solution.py:46
  554.5 18.0 %collective-permute-start.20 = (f32[5,8,1,128]{3,2,1,0:T(1,128)S(1)}, f32[5,8,1,128]{3,2,1,0:T(1,128)S(1)}, u32[]{:S(2)}, u32[]{:S(2)}) collective-permute-start(f32[5,8,1,128]{3,2,1,0:T(1,128)S(1)} %get-tuple-element.1226), channel_id=1, source_target_pairs={{4,0},{8,4},{12,8},{16,12},{20,16},{24,20},{28,24},{0,28},{5,1},{9... | collective-permute-start | bytes 61448 | tf_op jit(solution)/shard_map/while/body/eval_jaxpr/ppermute | solution.py:49
  569.8 22.3 %collective-permute-start.16 = (f32[19,8,1,128]{3,2,1,0:T(1,128)}, f32[19,8,1,128]{3,2,1,0:T(1,128)}, u32[]{:S(2)}, u32[]{:S(2)}) collective-permute-start(f32[19,8,1,128]{3,2,1,0:T(1,128)} %get-tuple-element.1183), channel_id=1, source_target_pairs={{4,0},{8,4},{12,8},{16,12},{20,16},{24,20},{28,24},{0,28},{5,1},{9... | collective-permute-start | bytes 233480 | tf_op jit(solution)/shard_map/while/body/eval_jaxpr/ppermute | solution.py:49
  572.5 19.6 %collective-permute-start.17 = (f32[19,8,1,128]{3,2,1,0:T(1,128)}, f32[19,8,1,128]{3,2,1,0:T(1,128)}, u32[]{:S(2)}, u32[]{:S(2)}) collective-permute-start(f32[19,8,1,128]{3,2,1,0:T(1,128)} %get-tuple-element.1184), channel_id=1, source_target_pairs={{0,4},{4,8},{8,12},{12,16},{16,20},{20,24},{24,28},{28,0},{1,5},{5... | collective-permute-start | bytes 233480 | tf_op jit(solution)/shard_map/while/body/eval_jaxpr/ppermute | solution.py:46
  696.6 17.9 %collective-permute-start.20 = (f32[5,8,1,128]{3,2,1,0:T(1,128)S(1)}, f32[5,8,1,128]{3,2,1,0:T(1,128)S(1)}, u32[]{:S(2)}, u32[]{:S(2)}) collective-permute-start(f32[5,8,1,128]{3,2,1,0:T(1,128)S(1)} %get-tuple-element.1226), channel_id=1, source_target_pairs={{4,0},{8,4},{12,8},{16,12},{20,16},{24,20},{28,24},{0,28},{5,1},{9... | collective-permute-start | bytes 61448 | tf_op jit(solution)/shard_map/while/body/eval_jaxpr/ppermute | solution.py:49
  711.8 22.3 %collective-permute-start.16 = (f32[19,8,1,128]{3,2,1,0:T(1,128)}, f32[19,8,1,128]{3,2,1,0:T(1,128)}, u32[]{:S(2)}, u32[]{:S(2)}) collective-permute-start(f32[19,8,1,128]{3,2,1,0:T(1,128)} %get-tuple-element.1183), channel_id=1, source_target_pairs={{4,0},{8,4},{12,8},{16,12},{20,16},{24,20},{28,24},{0,28},{5,1},{9... | collective-permute-start | bytes 233480 | tf_op jit(solution)/shard_map/while/body/eval_jaxpr/ppermute | solution.py:49
  714.5 19.7 %collective-permute-start.17 = (f32[19,8,1,128]{3,2,1,0:T(1,128)}, f32[19,8,1,128]{3,2,1,0:T(1,128)}, u32[]{:S(2)}, u32[]{:S(2)}) collective-permute-start(f32[19,8,1,128]{3,2,1,0:T(1,128)} %get-tuple-element.1184), channel_id=1, source_target_pairs={{0,4},{4,8},{8,12},{12,16},{16,20},{20,24},{24,28},{28,0},{1,5},{5... | collective-permute-start | bytes 233480 | tf_op jit(solution)/shard_map/while/body/eval_jaxpr/ppermute | solution.py:46
  838.6 18.0 %collective-permute-start.20 = (f32[5,8,1,128]{3,2,1,0:T(1,128)S(1)}, f32[5,8,1,128]{3,2,1,0:T(1,128)S(1)}, u32[]{:S(2)}, u32[]{:S(2)}) collective-permute-start(f32[5,8,1,128]{3,2,1,0:T(1,128)S(1)} %get-tuple-element.1226), channel_id=1, source_target_pairs={{4,0},{8,4},{12,8},{16,12},{20,16},{24,20},{28,24},{0,28},{5,1},{9... | collective-permute-start | bytes 61448 | tf_op jit(solution)/shard_map/while/body/eval_jaxpr/ppermute | solution.py:49
  853.9 22.3 %collective-permute-start.16 = (f32[19,8,1,128]{3,2,1,0:T(1,128)}, f32[19,8,1,128]{3,2,1,0:T(1,128)}, u32[]{:S(2)}, u32[]{:S(2)}) collective-permute-start(f32[19,8,1,128]{3,2,1,0:T(1,128)} %get-tuple-element.1183), channel_id=1, source_target_pairs={{4,0},{8,4},{12,8},{16,12},{20,16},{24,20},{28,24},{0,28},{5,1},{9... | collective-permute-start | bytes 233480 | tf_op jit(solution)/shard_map/while/body/eval_jaxpr/ppermute | solution.py:49
  856.6 19.6 %collective-permute-start.17 = (f32[19,8,1,128]{3,2,1,0:T(1,128)}, f32[19,8,1,128]{3,2,1,0:T(1,128)}, u32[]{:S(2)}, u32[]{:S(2)}) collective-permute-start(f32[19,8,1,128]{3,2,1,0:T(1,128)} %get-tuple-element.1184), channel_id=1, source_target_pairs={{0,4},{4,8},{8,12},{12,16},{16,20},{20,24},{24,28},{28,0},{1,5},{5... | collective-permute-start | bytes 233480 | tf_op jit(solution)/shard_map/while/body/eval_jaxpr/ppermute | solution.py:46
  980.7 17.9 %collective-permute-start.20 = (f32[5,8,1,128]{3,2,1,0:T(1,128)S(1)}, f32[5,8,1,128]{3,2,1,0:T(1,128)S(1)}, u32[]{:S(2)}, u32[]{:S(2)}) collective-permute-start(f32[5,8,1,128]{3,2,1,0:T(1,128)S(1)} %get-tuple-element.1226), channel_id=1, source_target_pairs={{4,0},{8,4},{12,8},{16,12},{20,16},{24,20},{28,24},{0,28},{5,1},{9... | collective-permute-start | bytes 61448 | tf_op jit(solution)/shard_map/while/body/eval_jaxpr/ppermute | solution.py:49
  995.9 22.3 %collective-permute-start.16 = (f32[19,8,1,128]{3,2,1,0:T(1,128)}, f32[19,8,1,128]{3,2,1,0:T(1,128)}, u32[]{:S(2)}, u32[]{:S(2)}) collective-permute-start(f32[19,8,1,128]{3,2,1,0:T(1,128)} %get-tuple-element.1183), channel_id=1, source_target_pairs={{4,0},{8,4},{12,8},{16,12},{20,16},{24,20},{28,24},{0,28},{5,1},{9... | collective-permute-start | bytes 233480 | tf_op jit(solution)/shard_map/while/body/eval_jaxpr/ppermute | solution.py:49
  998.6 19.7 %collective-permute-start.17 = (f32[19,8,1,128]{3,2,1,0:T(1,128)}, f32[19,8,1,128]{3,2,1,0:T(1,128)}, u32[]{:S(2)}, u32[]{:S(2)}) collective-permute-start(f32[19,8,1,128]{3,2,1,0:T(1,128)} %get-tuple-element.1184), channel_id=1, source_target_pairs={{0,4},{4,8},{8,12},{12,16},{16,20},{20,24},{24,28},{28,0},{1,5},{5... | collective-permute-start | bytes 233480 | tf_op jit(solution)/shard_map/while/body/eval_jaxpr/ppermute | solution.py:46
  1122.8 17.9 %collective-permute-start.20 = (f32[5,8,1,128]{3,2,1,0:T(1,128)S(1)}, f32[5,8,1,128]{3,2,1,0:T(1,128)S(1)}, u32[]{:S(2)}, u32[]{:S(2)}) collective-permute-start(f32[5,8,1,128]{3,2,1,0:T(1,128)S(1)} %get-tuple-element.1226), channel_id=1, source_target_pairs={{4,0},{8,4},{12,8},{16,12},{20,16},{24,20},{28,24},{0,28},{5,1},{9... | collective-permute-start | bytes 61448 | tf_op jit(solution)/shard_map/while/body/eval_jaxpr/ppermute | solution.py:49
  1138.0 22.3 %collective-permute-start.16 = (f32[19,8,1,128]{3,2,1,0:T(1,128)}, f32[19,8,1,128]{3,2,1,0:T(1,128)}, u32[]{:S(2)}, u32[]{:S(2)}) collective-permute-start(f32[19,8,1,128]{3,2,1,0:T(1,128)} %get-tuple-element.1183), channel_id=1, source_target_pairs={{4,0},{8,4},{12,8},{16,12},{20,16},{24,20},{28,24},{0,28},{5,1},{9... | collective-permute-start | bytes 233480 | tf_op jit(solution)/shard_map/while/body/eval_jaxpr/ppermute | solution.py:49
  1140.7 19.6 %collective-permute-start.17 = (f32[19,8,1,128]{3,2,1,0:T(1,128)}, f32[19,8,1,128]{3,2,1,0:T(1,128)}, u32[]{:S(2)}, u32[]{:S(2)}) collective-permute-start(f32[19,8,1,128]{3,2,1,0:T(1,128)} %get-tuple-element.1184), channel_id=1, source_target_pairs={{0,4},{4,8},{8,12},{12,16},{16,20},{20,24},{24,28},{28,0},{1,5},{5... | collective-permute-start | bytes 233480 | tf_op jit(solution)/shard_map/while/body/eval_jaxpr/ppermute | solution.py:46
  (635 other events, 5350.7 us)
where the time goes:
time: 1200 us
  waiting for transfers between devices  275 us (23%)
  local copies, waits for them, and re-layouts  262 us (22%)
  starting transfers between devices  256 us (21%)
  other arithmetic  226 us (19%)
  matrix products  144 us (12%)
  loops' own time  31.3 us (3%)
    ppermute x98, starting transfers between devices, with_halo(): lax.ppermute(lax.slice_in_dim(block, 0, width, axis=dim), axis, backward)  219 us
    ppermute x98, waiting for transfers between devices, with_halo(): lax.ppermute(lax.slice_in_dim(block, block.shape[dim] - width, None, axis...  208 us
    slice x73, local copies, waits for them, and re-layouts, with_halo(): lax.slice_in_dim(block, block.shape[dim] - width, None, axis=dim)  87 us
    ppermute x98, waiting for transfers between devices, with_halo(): lax.ppermute(lax.slice_in_dim(block, 0, width, axis=dim), axis, backward)  67.6 us
    concatenate x58, other arithmetic, with_halo(): block = jnp.concatenate([low, block, high], axis=dim)  66 us
    slice x48, local copies, waits for them, and re-layouts, with_halo(): lax.slice_in_dim(block, 0, width, axis=dim)  43.5 us
    ppermute x16, local copies, waits for them, and re-layouts, with_halo(): lax.ppermute(lax.slice_in_dim(block, block.shape[dim] - width, None, axis...  42.3 us
    ppermute x98, starting transfers between devices, with_halo(): lax.ppermute(lax.slice_in_dim(block, block.shape[dim] - width, None, axis...  37.2 us
  transfers between devices with their start and end apart: 196, of which 122 were waited for; matrix products, arithmetic and copies ran while one was open for 33% of the time, Pallas kernels for 0%

commit v1 on v0

v1 whole, which is shorter than its diff:
```python
import functools

import jax
import jax.numpy as jnp
import numpy as np
from jax import lax
from jax.experimental import pallas as pl
from jax.experimental.pallas import tpu as pltpu
from jax.sharding import PartitionSpec as P

STEPS = 8
SWEEPS = 3
FORCE_SCALE = 0.02
EXT_FIELD = 0.05
MESH = pl.DeviceIdType.MESH

VELOCITIES = [
    (0, 0, 0), (1, 0, 0), (-1, 0, 0), (0, 1, 0), (0, -1, 0), (0, 0, 1), (0, 0, -1),
    (1, 1, 0), (-1, -1, 0), (1, -1, 0), (-1, 1, 0), (1, 0, 1), (-1, 0, -1), (1, 0, -1),
    (-1, 0, 1), (0, 1, 1), (0, -1, -1), (0, 1, -1), (0, -1, 1),
]
OPPOSITE = [0] + [q + 1 if q % 2 else q - 1 for q in range(1, 19)]
X_UP, X_DOWN = (1, 7, 9, 11, 13), (2, 8, 10, 12, 14)
Y_UP, Y_DOWN = (3, 7, 10, 15, 17), (4, 8, 9, 16, 18)
DIAGONALS = ((1, 1), (1, -1), (-1, -1), (-1, 1))
LANES = 128


def isotropic(rates):
    rows = np.array([[1.0, 1.0, 1.0], [-30.0, -11.0, 8.0], [12.0, -4.0, 1.0]])
    count = np.array([1.0, 6.0, 12.0])
    weight = np.array([1.0 / 3.0, 1.0 / 18.0, 1.0 / 36.0])
    norm = np.sum(rows * rows * count[None, :], axis=1)
    strength = (1.0, rates[0], rates[1])
    return [
        [
            sum(
                float(rows[k, i] * rows[k, j] * weight[j] / (weight[i] * norm[k])) * strength[k]
                for k in range(3)
            )
            for j in range(3)
        ]
        for i in range(3)
    ]


def kernel(
    nx, ny, tx,
    rates_ref, diff_ref, bead_ref,
    pop_in, conc_in, pot_in, eps_in, solid_in, label_in,
    f_ref, conc_out, pot_out,
    post, pot, cc, velx, vely, velz, charge, scaled, wts, inv, bead, open_x, eps_x,
    face_x, face_y, face_z, face_left, bits,
    xs, xr, ys, yr, dr, pys, pyr,
    xs_sem, xr_sem, ys_sem, yr_sem, ds_sem, dr_sem,
    pxs_sem, pxr_sem, pys_sem, pyr_sem,
):
    mx, my = lax.axis_index("gx"), lax.axis_index("gy")
    up_x, down_x = lax.rem(mx + 1, nx), lax.rem(mx + nx - 1, nx)
    up_y, down_y = lax.rem(my + 1, ny), lax.rem(my + ny - 1, ny)
    to_x = ((up_x, my), (down_x, my))
    to_y = ((mx, up_y), (mx, down_y))
    to_diag = tuple(
        (up_x if dx > 0 else down_x, up_y if dy > 0 else down_y) for dx, dy in DIAGONALS
    )
    lane = lax.broadcasted_iota(jnp.int32, (8, LANES), 1)
    first, last = lane == 0, lane == LANES - 1

    barrier = pltpu.get_barrier_semaphore()
    for target in to_x + to_y + to_diag:
        pl.semaphore_signal(barrier, inc=1, device_id=target, device_id_type=MESH)
    pl.semaphore_wait(barrier, 8)

    def loop(body, carry, unroll):
        def outer(i, carry):
            for u in range(unroll):
                carry = body(i * unroll + u, carry)
            return carry

        return lax.fori_loop(0, tx // unroll, outer, carry)

    def roll(value, shift, axis):
        return pltpu.roll(value, shift, axis)

    def z_next(value):
        return roll(value, 7, 0)

    def z_prev(value):
        return roll(value, 1, 0)

    def y_prev(value, row, packed):
        return jnp.where(
            first, roll(packed, lax.rem(LANES - row, LANES), 1), roll(value, 1, 1)
        )

    def y_next(value, row, packed):
        return jnp.where(last, roll(packed, LANES - 1 - row, 1), roll(value, LANES - 1, 1))

    def pack_high(total, value, row):
        return jnp.where(lane == row, roll(value, row + 1, 1), total)

    def pack_low(total, value, row):
        return jnp.where(lane == row, roll(value, row, 1), total)

    def remote(source, target, send, receive, device):
        return pltpu.make_async_remote_copy(
            src_ref=source, dst_ref=target, send_sem=send, recv_sem=receive,
            device_id=device, device_id_type=MESH,
        )

    def x_copies(par):
        made = [
            remote(xs.at[d], xr.at[par, d], xs_sem.at[d], xr_sem.at[par, d], to_x[d])
            for d in range(2)
        ]
        for k, (dx, dy) in enumerate(DIAGONALS):
            source = xs.at[0 if dx > 0 else 1, 1 if dx == dy else 2]
            made.append(
                remote(source, dr.at[par, k], ds_sem.at[k], dr_sem.at[par, k], to_diag[k])
            )
        return made

    def y_copies(par):
        return [
            remote(ys.at[d], yr.at[par, d], ys_sem.at[d], yr_sem.at[par, d], to_y[d])
            for d in range(2)
        ]

    def pot_copies(b):
        made = [
            remote(pot.at[b, tx], pot.at[b, 0], pxs_sem.at[0], pxr_sem.at[b, 0], to_x[0]),
            remote(pot.at[b, 1], pot.at[b, tx + 1], pxs_sem.at[1], pxr_sem.at[b, 1], to_x[1]),
        ]
        for d in range(2):
            made.append(
                remote(pys.at[d], pyr.at[b, d], pys_sem.at[d], pyr_sem.at[b, d], to_y[d])
            )
        return made

    def with_corner(packed, par, k):
        dx, dy = DIAGONALS[k]
        spot = LANES - 1 if dx > 0 else tx
        shift = (spot - (LANES - 1 if dy > 0 else 0)) % LANES
        corner = dr[par, k]
        if shift:
            corner = roll(corner, shift, 1)
        return jnp.where(lane == spot, corner, packed)

    zero = jnp.zeros((8, LANES), jnp.float32)

    def begin(x, carry):
        acc = list(carry)
        opened = (1 - solid_in[x]).astype(jnp.float32)
        open_x[x + 1] = opened
        eps = eps_in[x]
        eps_x[x + 1] = eps
        start = pot_in[x]
        pot[0, x + 1] = start
        label = label_in[x]
        field = zero
        for level in range(4):
            field = jnp.where(label == level + 1, bead_ref[level], field)
        bead[x] = field
        cation, anion = conc_in[0, x], conc_in[1, x]
        cc[0, x + 1] = cation
        cc[1, x + 1] = anion
        charge[x] = opened * (cation - anion) + field
        for q in range(19):
            f_ref[q, x] = pop_in[q, x]
        for k, value in enumerate((opened, eps, start)):
            acc[k] = pack_high(acc[k], value, x)
            acc[3 + k] = pack_low(acc[3 + k], value, x)
        return tuple(acc)

    acc = loop(begin, (zero,) * 6, 1)
    for d in range(2):
        row = tx if d == 0 else 1
        for k in range(3):
            xs[d, k] = open_x[row]
            ys[d, k] = acc[3 * d + k]
        xs[d, 3] = eps_x[row]
        xs[d, 4] = pot[0, row]
        for k in range(5, 8):
            xs[d, k] = zero
        for k in range(3, 8):
            ys[d, k] = zero
        pys[d] = acc[3 * d + 2]
    moving = x_copies(1) + y_copies(1)
    for copy in moving:
        copy.start()
    for copy in moving:
        copy.wait()
    for d in range(2):
        row = 0 if d == 0 else tx + 1
        open_x[row] = xr[1, d, 0]
        eps_x[row] = xr[1, d, 3]
        pot[0, row] = xr[1, d, 4]
        pyr[0, d] = yr[1, d, 2]
    open_low = with_corner(with_corner(yr[1, 0, 0], 1, 0), 1, 3)
    open_high = with_corner(with_corner(yr[1, 1, 0], 1, 1), 1, 2)
    eps_low, eps_high = yr[1, 0, 1], yr[1, 1, 1]
    face_left[...] = yr[1, 0, 0] * ys[1, 0]
    face_x[0] = open_x[0] * open_x[1]

    def prepare(x, carry):
        eps, opened = eps_x[x + 1], open_x[x + 1]
        near = (
            eps_x[x + 2], eps_x[x],
            y_next(eps, x, eps_high), y_prev(eps, x, eps_low),
            z_next(eps), z_prev(eps),
        )
        near = [0.5 * (eps + other) for other in near]
        total = near[0] + near[1] + near[2] + near[3] + near[4] + near[5]
        whole = 1.0 / total
        inv[x] = whole
        for k in range(6):
            wts[k, x] = near[k] * whole
        scaled[x] = charge[x] * whole
        face_x[x + 1] = opened * open_x[x + 2]
        face_y[x] = opened * y_next(opened, x, open_high)
        face_z[x] = opened * z_next(opened)
        found = jnp.zeros((8, LANES), jnp.int32)
        for q in range(1, 19):
            sx, sy, sz = VELOCITIES[q]
            source = open_x[x - sx + 1]
            if sy > 0:
                source = y_prev(source, x - sx, open_low)
            elif sy < 0:
                source = y_next(source, x - sx, open_high)
            if sz:
                source = roll(source, sz % 8, 0)
            found = found + jnp.where(source > 0.5, 1 << q, 0)
        bits[x] = jnp.where(opened > 0.5, found, 0)
        return carry

    loop(prepare, 0, 1)

    rates = [rates_ref[k] for k in range(5)]
    iso = isotropic(rates)
    shear, ghost, heat, third = rates[3], rates[1], rates[2], rates[4]

    def deviator(n_shear, n_ghost):
        a, b = shear * (1.0 / n_shear), ghost * (1.0 / n_ghost)
        return (a + 4.0 * b, 0.5 * a - b, 2.0 * a - 4.0 * b, a + b)

    dev_x, dev_w = deviator(36.0, 72.0), deviator(12.0, 24.0)
    shear_off = 0.25 * shear
    odd = (0.1 + 0.4 * heat, 0.05 - 0.05 * heat, 0.2 - 0.2 * heat, 0.1 + 0.025 * heat)
    third_off = 0.125 * third
    spread = (diff_ref[0], diff_ref[1])

    def sweep(n):
        old, new = lax.rem(n, 2), lax.rem(n + 1, 2)
        low, high = pyr[old, 0], pyr[old, 1]

        def body(x, carry):
            here = pot[old, x + 1]
            value = scaled[x] + wts[0, x] * pot[old, x + 2] + wts[1, x] * pot[old, x]
            value = value + wts[2, x] * y_next(here, x, high) + wts[3, x] * y_prev(here, x, low)
            value = value + (wts[4, x] * z_next(here) + wts[5, x] * z_prev(here))
            pot[new, x + 1] = value
            return pack_high(carry[0], value, x), pack_low(carry[1], value, x)

        ends = loop(body, (zero, zero), 8)
        pys[0] = ends[0]
        pys[1] = ends[1]
        moving = pot_copies(new)
        for copy in moving:
            copy.start()
        for copy in moving:
            copy.wait()

    def collide(b):
        low, high = pyr[b, 0], pyr[b, 1]

        def body(x, carry):
            f = [f_ref[q, x] for q in range(19)]
            opened = open_x[x + 1]
            here = pot[b, x + 1]
            strength = (-0.5 * FORCE_SCALE) * (charge[x] * opened)
            fx = strength * (pot[b, x + 2] - pot[b, x])
            fy = strength * (y_next(here, x, high) - y_prev(here, x, low))
            fz = strength * (z_next(here) - z_prev(here) - 2.0 * EXT_FIELD)
            s = {q: f[q] + f[q + 1] for q in range(1, 19, 2)}
            d = {q: f[q] - f[q + 1] for q in range(1, 19, 2)}
            axis_sum = s[1] + s[3] + s[5]
            diag_sum = (s[7] + s[9]) + (s[11] + s[13]) + (s[15] + s[17])
            rho = (1.0 / 3.0) * f[0] + (1.0 / 18.0) * axis_sum + (1.0 / 36.0) * diag_sum
            hx, kx = d[7] + d[9], d[11] + d[13]
            hy, ky = d[7] - d[9], d[15] + d[17]
            hz, kz = d[11] - d[13], d[15] - d[17]
            momx = (1.0 / 18.0) * d[1] + (1.0 / 36.0) * (hx + kx) + 0.5 * fx
            momy = (1.0 / 18.0) * d[3] + (1.0 / 36.0) * (hy + ky) + 0.5 * fy
            momz = (1.0 / 18.0) * d[5] + (1.0 / 36.0) * (hz + kz) + 0.5 * fz
            over = 1.0 / rho
            ux, uy, uz = momx * over, momy * over, momz * over
            velx[x + 1] = ux
            vely[x] = uy
            velz[x] = uz
            work = ux * fx + uy * fy + uz * fz
            s0 = -3.0 * work
            k0 = s0 - 2.0 * rho + 3.0 * (momx * ux + momy * uy + momz * uz)
            wx, wy, wz = 9.0 * (fx - momx), 9.0 * (fy - momy), 9.0 * (fz - momz)
            gx, gy, gz = 3.0 * fx - 6.0 * momx, 3.0 * fy - 6.0 * momy, 3.0 * fz - 6.0 * momz
            nfx, nfy, nfz = 9.0 * fx, 9.0 * fy, 9.0 * fz

            def along(a, b, c):
                return {1: a, 3: b, 5: c, 7: a + b, 9: a - b, 11: a + c, 13: a - c, 15: b + c, 17: b - c}

            cu, cw, cf = along(ux, uy, uz), along(wx, wy, wz), along(nfx, nfy, nfz)
            xsum = {q: s[q] + k0 + cu[q] * cw[q] for q in s}
            src = {q: s0 + cu[q] * cf[q] for q in s}
            x0 = f[0] + 0.5 * k0
            bxy, cxy = xsum[7] + xsum[9], xsum[7] - xsum[9]
            bxz, cxz = xsum[11] + xsum[13], xsum[11] - xsum[13]
            byz, cyz = xsum[15] + xsum[17], xsum[15] - xsum[17]
            a_all = xsum[1] + xsum[3] + xsum[5]
            b_all = bxy + bxz + byz
            t0, t1, t2 = [r[0] * x0 + r[1] * a_all + r[2] * b_all for r in iso]
            p1, q1 = 3.0 * xsum[1] - a_all, b_all - 3.0 * byz
            p2, q2 = xsum[3] - xsum[5], bxy - bxz
            u1, u2 = dev_x[0] * p1 + dev_x[1] * q1, dev_x[2] * p1 + dev_x[3] * q1
            v1, v2 = dev_w[0] * p2 + dev_w[1] * q2, dev_w[2] * p2 + dev_w[3] * q2
            low1, low2 = t1 - u1, t2 + u2
            exy, exz, eyz = low2 + v2, low2 - v2, t2 - 2.0 * u2
            gxy, gxz, gyz = shear_off * cxy, shear_off * cxz, shear_off * cyz
            even = {
                1: t1 + 2.0 * u1, 3: low1 + v1, 5: low1 - v1,
                7: exy + gxy, 9: exy - gxy, 11: exz + gxz, 13: exz - gxz,
                15: eyz + gyz, 17: eyz - gyz,
            }

            def odd_part(d1, h, k, g, force):
                d1 = d1 + g
                both = h + k + 4.0 * g
                edge = 3.0 * force
                shared = edge - (odd[2] * d1 + odd[3] * both)
                turn = third_off * (h - k)
                return edge - (odd[0] * d1 + odd[1] * both), shared - turn, shared + turn

            ox, px, nxx = odd_part(d[1], hx, kx, gx, fx)
            oy, py, nyy = odd_part(d[3], hy, ky, gy, fy)
            oz, pz, nzz = odd_part(d[5], hz, kz, gz, fz)
            odds = {
                1: ox, 3: oy, 5: oz, 7: px + py, 9: px - py,
                11: nxx + pz, 13: nxx - pz, 15: nyy + nzz, 17: nyy - nzz,
            }
            is_open = opened > 0.5
            post[0, x + 1] = jnp.where(is_open, f[0] + s0 - t0, f[0])
            for q in range(1, 19, 2):
                ev = src[q] - even[q]
                post[q, x + 1] = jnp.where(is_open, f[q] + (ev + odds[q]), f[q + 1])
                post[q + 1, x + 1] = jnp.where(is_open, f[q + 1] + (ev - odds[q]), f[q])
            return carry

        loop(body, 0, 1)

    def pack_edges(x, carry):
        acc = list(carry)
        ions = (cc[0, x + 1], cc[1, x + 1], vely[x])
        for k in range(8):
            acc[k] = pack_high(acc[k], ions[k - 5] if k > 4 else post[Y_UP[k], x + 1], x)
        for k in range(8):
            acc[8 + k] = pack_low(acc[8 + k], ions[k - 5] if k > 4 else post[Y_DOWN[k], x + 1], x)
        return tuple(acc)

    def face_flux(a, b, vbar, drift, face, species):
        middle = 0.5 * (a + b)
        flow = middle * drift
        slope = b - a
        slope = slope + flow if species == 0 else slope - flow
        return (vbar * middle - spread[species] * slope) * face

    def transport(par, b):
        ends = [
            face_flux(
                yr[par, 0, 5 + k], ys[1, 5 + k], 0.5 * (yr[par, 0, 7] + ys[1, 7]),
                pys[1] - pyr[b, 0], face_left[...], k,
            )
            for k in range(2)
        ]
        pot_high, vel_high = pyr[b, 1], yr[par, 1, 7]
        conc_high = (yr[par, 1, 5], yr[par, 1, 6])
        below = tuple(
            face_flux(
                cc[k, 0], cc[k, 1], 0.5 * (velx[0] + velx[1]),
                pot[b, 1] - pot[b, 0], face_x[0], k,
            )
            for k in range(2)
        )

        def body(x, below):
            here = pot[b, x + 1]
            drift_x = pot[b, x + 2] - here
            drift_y = y_next(here, x, pot_high) - here
            drift_z = z_next(here) - here - EXT_FIELD
            vy, vz = vely[x], velz[x]
            vbar_x = 0.5 * (velx[x + 1] + velx[x + 2])
            vbar_y = 0.5 * (vy + y_next(vy, x, vel_high))
            vbar_z = 0.5 * (vz + z_next(vz))
            above, fresh = [], []
            for k in range(2):
                c = cc[k, x + 1]
                up = face_flux(c, cc[k, x + 2], vbar_x, drift_x, face_x[x + 1], k)
                side = face_flux(c, y_next(c, x, conc_high[k]), vbar_y, drift_y, face_y[x], k)
                deep = face_flux(c, z_next(c), vbar_z, drift_z, face_z[x], k)
                change = (up - below[k]) + (side - y_prev(side, x, ends[k])) + (deep - z_prev(deep))
                above.append(up)
                fresh.append(c - change)
            cc[0, x + 1] = fresh[0]
            cc[1, x + 1] = fresh[1]
            total = open_x[x + 1] * (fresh[0] - fresh[1]) + bead[x]
            charge[x] = total
            scaled[x] = total * inv[x]
            return tuple(above)

        loop(body, below, 2)

    def stream(par):
        low = {q: yr[par, 0, k] for k, q in enumerate(Y_UP)}
        high = {q: yr[par, 1, k] for k, q in enumerate(Y_DOWN)}
        low[7] = with_corner(low[7], par, 0)
        high[9] = with_corner(high[9], par, 1)
        high[8] = with_corner(high[8], par, 2)
        low[10] = with_corner(low[10], par, 3)

        def body(x, carry):
            mask = bits[x]
            f_ref[0, x] = post[0, x + 1]
            for q in range(1, 19):
                sx, sy, sz = VELOCITIES[q]
                value = post[q, x - sx + 1]
                if sy > 0:
                    value = y_prev(value, x - sx, low[q])
                elif sy < 0:
                    value = y_next(value, x - sx, high[q])
                if sz:
                    value = roll(value, sz % 8, 0)
                f_ref[q, x] = jnp.where((mask & (1 << q)) != 0, value, post[OPPOSITE[q], x + 1])
            return carry

        loop(body, 0, 1)

    def step(t, carry):
        par = lax.rem(t, 2)

        def one(k, carry):
            sweep(t * SWEEPS + k)
            return carry

        lax.fori_loop(0, SWEEPS, one, 0)
        b = lax.rem((t + 1) * SWEEPS, 2)
        collide(b)
        for d in range(2):
            row = tx if d == 0 else 1
            for k, q in enumerate((X_UP, X_DOWN)[d]):
                xs[d, k] = post[q, row]
            xs[d, 5] = cc[0, row]
            xs[d, 6] = cc[1, row]
            xs[d, 7] = velx[row]
        across = x_copies(par)
        for copy in across:
            copy.start()
        acc = loop(pack_edges, (zero,) * 16, 2)
        for d in range(2):
            for k in range(8):
                ys[d, k] = acc[8 * d + k]
        sideways = y_copies(par)
        for copy in sideways:
            copy.start()
        for copy in across + sideways:
            copy.wait()
        for d in range(2):
            row = 0 if d == 0 else tx + 1
            for k, q in enumerate((X_UP, X_DOWN)[d]):
                post[q, row] = xr[par, d, k]
            cc[0, row] = xr[par, d, 5]
            cc[1, row] = xr[par, d, 6]
            velx[row] = xr[par, d, 7]
        transport(par, b)
        stream(par)
        return carry

    lax.fori_loop(0, STEPS, step, 0)

    def finish(x, carry):
        conc_out[0, x] = cc[0, x + 1]
        conc_out[1, x] = cc[1, x + 1]
        pot_out[x] = pot[(STEPS * SWEEPS) % 2, x + 1]
        return carry

    loop(finish, 0, 1)


def local(nx, ny, populations, concentrations, potential, permittivity, solid, bead_label,
          bead_charge, rates, diffusivity):
    tx = populations.shape[2]

    def turn(array):
        return jnp.swapaxes(array, -3, -2)

    f32 = jnp.float32
    tile = (8, LANES)

    def vmem(*lead):
        return pltpu.VMEM(lead + tile, f32)

    dma = pltpu.SemaphoreType.DMA
    smem = pl.BlockSpec(memory_space=pltpu.SMEM)
    block = pl.BlockSpec(memory_space=pltpu.VMEM)
    outs = pl.pallas_call(
        functools.partial(kernel, nx, ny, tx),
        out_shape=[
            jax.ShapeDtypeStruct((19, tx) + tile, f32),
            jax.ShapeDtypeStruct((2, tx) + tile, f32),
            jax.ShapeDtypeStruct((tx,) + tile, f32),
        ],
        in_specs=[smem] * 3 + [block] * 6,
        out_specs=[block] * 3,
        scratch_shapes=[
            vmem(19, tx + 2), vmem(2, tx + 2), vmem(2, tx + 2), vmem(tx + 2), vmem(tx), vmem(tx),
            vmem(tx), vmem(tx), vmem(6, tx), vmem(tx), vmem(tx), vmem(tx + 2), vmem(tx + 2),
            vmem(tx + 1), vmem(tx), vmem(tx), vmem(), pltpu.VMEM((tx,) + tile, jnp.int32),
            vmem(2, 8), vmem(2, 2, 8), vmem(2, 8), vmem(2, 2, 8), vmem(2, 4), vmem(2), vmem(2, 2),
            dma((2,)), dma((2, 2)), dma((2,)), dma((2, 2)), dma((4,)), dma((2, 4)),
            dma((2,)), dma((2, 2)), dma((2,)), dma((2, 2)),
        ],
        compiler_params=pltpu.CompilerParams(
            collective_id=0, has_side_effects=True, vmem_limit_bytes=48 * 1024 * 1024
        ),
    )(
        rates, diffusivity, bead_charge,
        turn(populations), turn(concentrations), turn(potential), turn(permittivity),
        turn(solid), turn(bead_label),
    )
    return tuple(turn(array) for array in outs)


def solution(mesh):
    in_specs = (
        P(None, None, "gx", "gy"),
        P(None, None, "gx", "gy"),
        P(None, "gx", "gy"),
        P(None, "gx", "gy"),
        P(None, "gx", "gy"),
        P(None, "gx", "gy"),
        P(),
        P(),
        P(),
    )
    out_specs = (P(None, None, "gx", "gy"), P(None, None, "gx", "gy"), P(None, "gx", "gy"))
    return jax.shard_map(
        functools.partial(local, mesh.shape["gx"], mesh.shape["gy"]),
        mesh=mesh, in_specs=in_specs, out_specs=out_specs, check_vma=False,
    )
```

time: 1200 us -> 298 us (0.25)
  Pallas kernels: 0 us -> 287 us
  waiting for transfers between devices: 275 us -> 0 us
  starting transfers between devices: 256 us -> 0 us
  local copies, waits for them, and re-layouts: 262 us -> 10.5 us
  other arithmetic: 226 us -> 0 us
  matrix products: 144 us -> 0 us
  loops' own time: 31.3 us -> 0 us
    pallas_call x0 -> x1, Pallas kernels: none -> 287 us  [local(): pl.pallas_call(functools.partial(kernel, nx, ny, tx), out_shape=[jax.Shap...]
    ppermute x196 -> x0, waiting for transfers between devices: 275 us -> none  [the longest x98 208 us: with_halo(): lax.ppermute(lax.slice_in_dim(block, block.shape[dim] - width, None, axis...]
    ppermute x196 -> x0, starting transfers between devices: 256 us -> none  [the longest x98 219 us: with_halo(): lax.ppermute(lax.slice_in_dim(block, 0, width, axis=dim), axis, backward)]
    slice x253 -> x0, local copies, waits for them, and re-layouts: 149 us -> none  [the longest x73 87 us: with_halo(): lax.slice_in_dim(block, block.shape[dim] - width, None, axis=dim)]
    dot_general x41 -> x0, matrix products: 144 us -> none  [the longest x8 34.7 us: macroscopic(): density = jnp.einsum('q,q...->...', weights, populations, precision=HIGHEST)]
    ppermute x32 -> x0, local copies, waits for them, and re-layouts: 79 us -> none  [the longest x16 42.3 us: with_halo(): lax.ppermute(lax.slice_in_dim(block, block.shape[dim] - width, None, axis...]
    concatenate x72 -> x0, other arithmetic: 69.9 us -> none  [the longest x58 66 us: with_halo(): block = jnp.concatenate([low, block, high], axis=dim)]
    sub x32 -> x0, other arithmetic: 43.8 us -> none  [the longest x16 19.7 us: face_flux(): drift = (next_pot - here_pot - bias)[None]]
  transfers between devices with their start and end apart: 196 -> 0, of which waited for: 122 -> 0; matrix products, arithmetic and copies ran while one was open for 33% -> 0% of each run, Pallas kernels for 0% -> 0%
where the time goes in v1:
time: 298 us
  Pallas kernels  287 us (96%)
  local copies, waits for them, and re-layouts  10.5 us (4%)
    pallas_call x1, Pallas kernels, local(): pl.pallas_call(functools.partial(kernel, nx, ny, tx), out_shape=[jax.Shap...  287 us
    unnamed x11, local copies, waits for them, and re-layouts  8.2 us

profile of v1, /device:TPU:0, one launch (start us, length us, event | category | flops | bytes accessed | tf_op | source)
XLA Modules:
  0.0 298.2 jit_solution(13696148232100056646)
XLA Ops:
  0.6 1.1 copy.28
  1.7 1.1 copy_bitcast_fusion.4
  2.9 1.1 copy_bitcast_fusion.2
  4.0 0.0 copy-start
  4.0 0.0 copy-start.1
  4.0 0.0 copy-start.2
  4.0 3.8 %copy.27 = f32[19,8,32,128]{3,1,2,0:T(8,128)S(1)} copy(f32[19,8,32,128]{3,2,1,0:T(8,128)} %param.9) | data formatting | bytes 4980736 | tf_op args[0]
  7.8 0.0 copy-done
  7.8 0.0 copy-done.1
  7.8 0.0 copy-done.2
  7.8 287.0 %shard_map.112 = (f32[19,32,8,128]{3,2,1,0:T(8,128)S(1)}, f32[2,32,8,128]{3,2,1,0:T(8,128)S(1)}, f32[32,8,128]{2,1,0:T(8,128)S(1)}) custom-call(f32[5]{0:T(128)S(1)} %copy-done, f32[2]{0:T(128)S(1)} %copy-done.1, f32[4]{0:T(128)S(1)} %copy-done.2, f32[19,32,8,128]{3,2,1,0:T(8,128)S(1)} %bitcast.17, f32[2,32,8,128]{3,2,1,0:T(8,128)S(1)} %bitcast.19, ...), custom_call_target="tpu_custom_call" | custom-call | tf_op jit(solution)/shard_map/pallas_call | solution.py:511
  294.9 1.9 copy.18
  296.8 0.8 copy.19
  297.5 0.7 copy.20
Async XLA Ops:
  4.0 3.8 %copy-start = (f32[5]{0:T(128)S(1)}, f32[5]{0:T(128)}, u32[]{:S(2)}) copy-start(f32[5]{0:T(128)} %rates_ref.1) | copy-start | bytes 64
  4.0 3.8 %copy-start.1 = (f32[2]{0:T(128)S(1)}, f32[2]{0:T(128)}, u32[]{:S(2)}) copy-start(f32[2]{0:T(128)} %diff_ref.1) | copy-start | bytes 28
  4.0 3.8 %copy-start.2 = (f32[4]{0:T(128)S(1)}, f32[4]{0:T(128)}, u32[]{:S(2)}) copy-start(f32[4]{0:T(128)} %bead_ref.1) | copy-start | bytes 52

commit v2 on v1

--- a/solution.py
+++ b/solution.py
@@ -166,7 +166,7 @@
         cc[1, x + 1] = anion
         charge[x] = opened * (cation - anion) + field
         for q in range(19):
-            f_ref[q, x] = pop_in[q, x]
+            post[OPPOSITE[q], x + 1] = pop_in[q, x]
         for k, value in enumerate((opened, eps, start)):
             acc[k] = pack_high(acc[k], value, x)
             acc[3 + k] = pack_low(acc[3 + k], value, x)
@@ -185,6 +185,8 @@
         for k in range(3, 8):
             ys[d, k] = zero
         pys[d] = acc[3 * d + 2]
+        for q in range(19):
+            post[q, 0 if d == 0 else tx + 1] = zero
     moving = x_copies(1) + y_copies(1)
     for copy in moving:
         copy.start()
@@ -249,7 +251,7 @@
     third_off = 0.125 * third
     spread = (diff_ref[0], diff_ref[1])
 
-    def sweep(n):
+    def sweep(n, meanwhile):
         old, new = lax.rem(n, 2), lax.rem(n + 1, 2)
         low, high = pyr[old, 0], pyr[old, 1]
 
@@ -261,12 +263,13 @@
             pot[new, x + 1] = value
             return pack_high(carry[0], value, x), pack_low(carry[1], value, x)
 
-        ends = loop(body, (zero, zero), 8)
+        ends = loop(body, (zero, zero), 16)
         pys[0] = ends[0]
         pys[1] = ends[1]
         moving = pot_copies(new)
         for copy in moving:
             copy.start()
+        meanwhile()
         for copy in moving:
             copy.wait()
 
@@ -353,7 +356,7 @@
                 post[q + 1, x + 1] = jnp.where(is_open, f[q + 1] + (ev - odds[q]), f[q])
             return carry
 
-        loop(body, 0, 1)
+        loop(body, 0, 2)
 
     def pack_edges(x, carry):
         acc = list(carry)
@@ -414,9 +417,9 @@
             scaled[x] = total * inv[x]
             return tuple(above)
 
-        loop(body, below, 2)
-
-    def stream(par):
+        loop(body, below, 4)
+
+    def stream(par, begun, start, stop):
         low = {q: yr[par, 0, k] for k, q in enumerate(Y_UP)}
         high = {q: yr[par, 1, k] for k, q in enumerate(Y_DOWN)}
         low[7] = with_corner(low[7], par, 0)
@@ -424,8 +427,8 @@
         high[8] = with_corner(high[8], par, 2)
         low[10] = with_corner(low[10], par, 3)
 
-        def body(x, carry):
-            mask = bits[x]
+        def body(x):
+            mask = jnp.where(begun, bits[x], 0)
             f_ref[0, x] = post[0, x + 1]
             for q in range(1, 19):
                 sx, sy, sz = VELOCITIES[q]
@@ -437,15 +440,22 @@
                 if sz:
                     value = roll(value, sz % 8, 0)
                 f_ref[q, x] = jnp.where((mask & (1 << q)) != 0, value, post[OPPOSITE[q], x + 1])
+
+        def rows(i, carry):
+            for u in range(4):
+                body(i * 4 + u)
             return carry
 
-        loop(body, 0, 1)
+        lax.fori_loop(start, stop, rows, 0)
+
+    groups = tx // 4
 
     def step(t, carry):
         par = lax.rem(t, 2)
 
         def one(k, carry):
-            sweep(t * SWEEPS + k)
+            start, stop = lax.div(k * groups, SWEEPS), lax.div((k + 1) * groups, SWEEPS)
+            sweep(t * SWEEPS + k, lambda: stream(1 - par, t > 0, start, stop))
             return carry
 
         lax.fori_loop(0, SWEEPS, one, 0)
@@ -461,7 +471,7 @@
         across = x_copies(par)
         for copy in across:
             copy.start()
-        acc = loop(pack_edges, (zero,) * 16, 2)
+        acc = loop(pack_edges, (zero,) * 16, 4)
         for d in range(2):
             for k in range(8):
                 ys[d, k] = acc[8 * d + k]
@@ -478,10 +488,10 @@
             cc[1, row] = xr[par, d, 6]
             velx[row] = xr[par, d, 7]
         transport(par, b)
-        stream(par)
         return carry
 
     lax.fori_loop(0, STEPS, step, 0)
+    stream((STEPS - 1) % 2, True, 0, groups)
 
     def finish(x, carry):
         conc_out[0, x] = cc[0, x + 1]

time: 298 us -> 248 us (0.83)
  Pallas kernels: 287 us -> 237 us
    pallas_call x1, Pallas kernels: 287 us -> 237 us  [local(): pl.pallas_call(functools.partial(kernel, nx, ny, tx), out_shape=[jax.Shap...]
where the time goes in v2:
time: 248 us
  Pallas kernels  237 us (96%)
  local copies, waits for them, and re-layouts  10.5 us (4%)
    pallas_call x1, Pallas kernels, local(): pl.pallas_call(functools.partial(kernel, nx, ny, tx), out_shape=[jax.Shap...  237 us
    unnamed x11, local copies, waits for them, and re-layouts  8.2 us

profile of v2, /device:TPU:0, one launch (start us, length us, event | category | flops | bytes accessed | tf_op | source)
XLA Modules:
  0.0 248.0 jit_solution(5065172019523892862)
XLA Ops:
  0.6 1.1 copy.28
  1.7 1.1 copy_bitcast_fusion.4
  2.9 1.1 copy_bitcast_fusion.2
  4.0 0.0 copy-start
  4.0 0.0 copy-start.1
  4.0 0.0 copy-start.2
  4.0 3.8 %copy.27 = f32[19,8,32,128]{3,1,2,0:T(8,128)S(1)} copy(f32[19,8,32,128]{3,2,1,0:T(8,128)} %param.9) | data formatting | bytes 4980736 | tf_op args[0]
  7.8 0.0 copy-done
  7.8 0.0 copy-done.1
  7.8 0.0 copy-done.2
  7.8 236.9 %shard_map.112 = (f32[19,32,8,128]{3,2,1,0:T(8,128)S(1)}, f32[2,32,8,128]{3,2,1,0:T(8,128)S(1)}, f32[32,8,128]{2,1,0:T(8,128)S(1)}) custom-call(f32[5]{0:T(128)S(1)} %copy-done, f32[2]{0:T(128)S(1)} %copy-done.1, f32[4]{0:T(128)S(1)} %copy-done.2, f32[19,32,8,128]{3,2,1,0:T(8,128)S(1)} %bitcast.17, f32[2,32,8,128]{3,2,1,0:T(8,128)S(1)} %bitcast.19, ...), custom_call_target="tpu_custom_call" | custom-call | tf_op jit(solution)/shard_map/pallas_call | solution.py:521
  244.7 1.9 copy.18
  246.6 0.8 copy.19
  247.4 0.7 copy.20
Async XLA Ops:
  4.0 3.8 %copy-start = (f32[5]{0:T(128)S(1)}, f32[5]{0:T(128)}, u32[]{:S(2)}) copy-start(f32[5]{0:T(128)} %rates_ref.1) | copy-start | bytes 64
  4.0 3.8 %copy-start.1 = (f32[2]{0:T(128)S(1)}, f32[2]{0:T(128)}, u32[]{:S(2)}) copy-start(f32[2]{0:T(128)} %diff_ref.1) | copy-start | bytes 28
  4.0 3.8 %copy-start.2 = (f32[4]{0:T(128)S(1)}, f32[4]{0:T(128)}, u32[]{:S(2)}) copy-start(f32[4]{0:T(128)} %bead_ref.1) | copy-start | bytes 52
